TPU v7x, 32 devices: a whole 2x2x4 slice. The times are simulated.
32 devices in a mesh: row: 4 (over z), col: 8 (over y, x, core).
Axes of the slice: x: 2, y: 2, z: 4, core: 2. Of those that a mesh axis runs over, the one named last changes fastest.
Arguments:
- scalars: float32 [1, 256, 256, 512], P(None, 'row', 'col'), may hold values from -6 to 6
- velocity: bfloat16 [3, 256, 256, 512], P(None, 'row', 'col'), may hold values from -6 to 6
- first_x: bfloat16 [512, 512], replicated, may hold values from -0.25 to 0.25
- second_x: bfloat16 [512, 512], replicated, may hold values from -0.25 to 0.25
- first_y: bfloat16 [256, 256], replicated, may hold values from -0.375 to 0.375
- second_y: bfloat16 [256, 256], replicated, may hold values from -0.375 to 0.375
- first_z: bfloat16 [256, 256], replicated, may hold values from -0.375 to 0.375
- second_z: bfloat16 [256, 256], replicated, may hold values from -0.375 to 0.375
Outputs:
- updated: float32 [1, 256, 256, 512], P(None, 'row', 'col')
All inputs are finite; a program needn't handle non-finite values.
Results may differ from a plain program's by a relative error of at most 0.0021.
Values may be sent and summed in bfloat16 or wider, within the bound.
A program may use at most 128 MiB of HBM per device.

v0:
```python
import functools

import jax
import jax.numpy as jnp
from jax import lax
from jax.experimental import pallas as pl
from jax.experimental.pallas import tpu as pltpu
from jax.sharding import PartitionSpec as P

diffusion_coefficient = 0.5
step_weight = 0.5
MESH = pl.DeviceIdType.MESH
LANES = 128

Y_CHUNKS = 4
Z_CHUNKS = 2


def contract_last(scalar_values, matrix):
    return lax.dot_general(
        scalar_values,
        matrix,
        (((scalar_values.ndim - 1,), (1,)), ((), ())),
        preferred_element_type=jnp.float32,
    )


def contract_middle(scalar_values, matrix):
    return jnp.einsum("syc,ky->skc", scalar_values, matrix, preferred_element_type=jnp.float32)


def derivative_pair(scalar_values, first_derivative_matrix, second_derivative_matrix, apply_matrix):
    return (
        apply_matrix(scalar_values, first_derivative_matrix),
        apply_matrix(scalar_values, second_derivative_matrix),
    )


def axis_contribution(
    scalar_values, velocity_field, first_derivative_matrix, second_derivative_matrix, apply_matrix
):
    velocity_flux = velocity_field.astype(jnp.float32)
    flux_product = (velocity_flux * scalar_values.astype(jnp.float32)).astype(jnp.bfloat16)
    scalar_gradient, second_derivative = derivative_pair(
        scalar_values, first_derivative_matrix, second_derivative_matrix, apply_matrix
    )
    advected_scalar = apply_matrix(flux_product, first_derivative_matrix)
    return (
        -0.5 * (velocity_flux * scalar_gradient + advected_scalar)
        + diffusion_coefficient * second_derivative
    )


def body(scalars, velocity, first_x, second_x, first_y, second_y, first_z, second_z):
    scalar_count = scalars.shape[0]
    rows_local = scalars.shape[1]
    depth_z = scalars.shape[2]
    length_x = scalars.shape[3]
    compiled_step = scalars.astype(jnp.bfloat16)
    x_term = axis_contribution(compiled_step, velocity[0], first_x, second_x, contract_last)
    turned = jnp.transpose(jnp.concatenate([compiled_step, velocity[1:]], axis=0), (0, 1, 3, 2))
    y_payload = turned[: scalar_count + 1].reshape(scalar_count + 1, rows_local, length_x * depth_z)
    z_payload = jnp.concatenate([turned[:scalar_count], turned[scalar_count + 1 :]], axis=0)
    pencil_y = lax.all_to_all(y_payload, "row", split_axis=2, concat_axis=1, tiled=True)
    pencil_z = lax.all_to_all(z_payload, "col", split_axis=2, concat_axis=3, tiled=True)
    y_term = axis_contribution(
        pencil_y[:scalar_count], pencil_y[scalar_count], first_y, second_y, contract_middle
    )
    z_term = axis_contribution(
        pencil_z[:scalar_count], pencil_z[scalar_count], first_z, second_z, contract_last
    )
    y_home = lax.all_to_all(y_term, "row", split_axis=1, concat_axis=2, tiled=True)
    z_home = lax.all_to_all(z_term, "col", split_axis=3, concat_axis=2, tiled=True)
    returned = y_home.reshape(scalar_count, rows_local, length_x, depth_z) + z_home
    returned = jnp.transpose(returned, (0, 1, 3, 2))
    return scalars + step_weight * (x_term + returned)


def pair_term(velocity, gradient, advected, second):
    half = 0.5 * step_weight
    return -half * (velocity * gradient + advected) + (step_weight * diffusion_coefficient) * second


def dot(a, b):
    return jnp.dot(a, b, preferred_element_type=jnp.float32)


def dot_rows(a, b):
    return lax.dot_general(a, b, (((1,), (1,)), ((), ())), preferred_element_type=jnp.float32)


def kernel(
    rows, cols, scal, vel, f1x, f2x, f1y, f2y, f1z, f2z, out,
    acc, vb, vf, turned, py, ysend, yhome, sw, ub, pz, zsend, zhome,
    m1x, m2x, m1y, m2y, m1z, m2z,
    in_sem, own_sem, yf_send, yf_recv, yr_send, yr_recv, zf_send, zf_recv, zr_send, zr_recv,
):
    my_row, my_col = lax.axis_index("row"), lax.axis_index("col")
    ylen, zlen, xlen = ub.shape
    blocks = xlen // LANES
    zc = zlen // Y_CHUNKS
    yb = ylen // cols
    yc = yb // Z_CHUNKS

    def row_of(d):
        return lax.rem(my_row + d, rows)

    def col_of(d):
        return lax.rem(my_col + d, cols)

    def lanes(b):
        return pl.ds(b * LANES, LANES)

    loads = []

    def load(src, dst):
        copy = pltpu.make_async_copy(src, dst, in_sem.at[len(loads)])
        copy.start()
        loads.append(copy)
        return copy

    scal_in = [load(scal.at[:, lanes(b)], acc.at[b]) for b in range(blocks)]
    v_in = [load(vel.at[1, :, :, lanes(b)], vb.at[b]) for b in range(blocks)]
    w_in = load(vel.at[2], sw.at[:, 1])
    u_in = load(vel.at[0], ub)
    x_in = [load(f1x, m1x), load(f2x, m2x)]
    y_in = [load(f1y, m1y), load(f2y, m2y)]
    z_in = [load(f1z, m1z), load(f2z, m2z)]

    barrier = pltpu.get_barrier_semaphore()
    for d in range(1, rows):
        pl.semaphore_signal(barrier, inc=1, device_id=(row_of(d), my_col), device_id_type=MESH)
    for d in range(1, cols):
        pl.semaphore_signal(barrier, inc=1, device_id=(my_row, col_of(d)), device_id_type=MESH)

    def y_forward(k, d, sender, receiver):
        zs = pl.ds(k * zc, zc)
        return pltpu.make_async_remote_copy(
            src_ref=turned.at[receiver, zs],
            dst_ref=py.at[zs, :, pl.ds(sender * ylen, ylen)],
            send_sem=yf_send.at[k, d - 1], recv_sem=yf_recv.at[k, d - 1],
            device_id=(row_of(d), my_col), device_id_type=MESH)

    def y_return(k, d, sender, receiver):
        zs = pl.ds(k * zc, zc)
        return pltpu.make_async_remote_copy(
            src_ref=ysend.at[zs, pl.ds(receiver * ylen, ylen)],
            dst_ref=yhome.at[sender, zs],
            send_sem=yr_send.at[k, d - 1], recv_sem=yr_recv.at[k, d - 1],
            device_id=(row_of(d), my_col), device_id_type=MESH)

    def z_forward(k, d, sender, receiver):
        return pltpu.make_async_remote_copy(
            src_ref=sw.at[pl.ds(receiver * yb + k * yc, yc)],
            dst_ref=pz.at[pl.ds(k * yc, yc), :, pl.ds(sender * zlen, zlen)],
            send_sem=zf_send.at[k, d - 1], recv_sem=zf_recv.at[k, d - 1],
            device_id=(my_row, col_of(d)), device_id_type=MESH)

    def z_return(k, d, sender, receiver):
        return pltpu.make_async_remote_copy(
            src_ref=zsend.at[pl.ds(k * yc, yc), pl.ds(receiver * zlen, zlen)],
            dst_ref=zhome.at[pl.ds(sender * yb + k * yc, yc)],
            send_sem=zr_send.at[k, d - 1], recv_sem=zr_recv.at[k, d - 1],
            device_id=(my_row, col_of(d)), device_id_type=MESH)

    def own_copy(src, dst, index):
        copy = pltpu.make_async_copy(src, dst, own_sem.at[index])
        copy.start()
        return copy

    for copy in scal_in + v_in:
        copy.wait()

    @pl.loop(0, ylen)
    def _(y):
        span = pl.ds(pl.multiple_of(y * zlen, zlen), zlen)
        for b in range(blocks):
            vf[b, span] = vb[b, y].astype(jnp.float32)

    own = {}
    sends = []

    def order(n):
        return range(n - 1, 0, -1)

    def turn_and_send_y(k):
        @pl.loop(k * zc, (k + 1) * zc)
        def _(z):
            for b in range(blocks):
                turned[b, z, 0] = acc[b, pl.ds(z, ylen, stride=zlen), :].astype(jnp.bfloat16)
                turned[b, z, 1] = vf[b, pl.ds(z, ylen, stride=zlen), :].astype(jnp.bfloat16)

        if k == 0:
            pl.semaphore_wait(barrier, rows + cols - 2)
        for d in order(rows):
            copy = y_forward(k, d, my_row, row_of(d))
            copy.start()
            sends.append(copy)
        zs = pl.ds(k * zc, zc)
        own["yf", k] = own_copy(
            turned.at[my_row, zs], py.at[zs, :, pl.ds(my_row * ylen, ylen)], k)

    turn_and_send_y(0)

    @pl.loop(0, ylen)
    def _(y):
        span = pl.ds(pl.multiple_of(y * zlen, zlen), zlen)
        for b in range(blocks):
            sw[y, 0, :, lanes(b)] = acc[b, span].astype(jnp.bfloat16)

    w_in.wait()
    for k in range(Z_CHUNKS):
        for d in order(cols):
            copy = z_forward(k, d, my_col, col_of(d))
            copy.start()
            sends.append(copy)
        own["zf", k] = own_copy(
            sw.at[pl.ds(my_col * yb + k * yc, yc)],
            pz.at[pl.ds(k * yc, yc), :, pl.ds(my_col * zlen, zlen)], Y_CHUNKS + k)
    for k in range(1, Y_CHUNKS):
        turn_and_send_y(k)

    u_in.wait()
    for copy in x_in:
        copy.wait()
    y_tile = max(1, 256 // zlen)
    while ylen % y_tile:
        y_tile -= 1
    tile = y_tile * zlen

    @pl.loop(0, ylen // y_tile)
    def _(i):
        ys = pl.ds(i * y_tile, y_tile)
        span = pl.ds(pl.multiple_of(i * tile, tile), tile)
        s = sw[ys, 0].reshape(tile, xlen)
        u = ub[ys].reshape(tile, xlen).astype(jnp.float32)
        flux = (u * s.astype(jnp.float32)).astype(jnp.bfloat16)
        term = pair_term(u, dot_rows(s, m1x[...]), dot_rows(flux, m1x[...]), dot_rows(s, m2x[...]))
        for b in range(blocks):
            acc[b, span] += term[:, b * LANES:(b + 1) * LANES]

    for copy in y_in + z_in:
        copy.wait()

    def y_terms(k):
        own["yf", k].wait()
        for d in order(rows):
            y_forward(k, d, row_of(rows - d), my_row).wait_recv()

        @pl.loop(k * zc, (k + 1) * zc)
        def _(z):
            s = py[z, 0]
            v = py[z, 1].astype(jnp.float32)
            flux = (v * s.astype(jnp.float32)).astype(jnp.bfloat16)
            both = dot(m1y[...], jnp.concatenate([s, flux], axis=1))
            term = pair_term(v, both[:, :LANES], both[:, LANES:], dot(m2y[...], s))
            ysend[z] = term.astype(jnp.bfloat16)

        for d in order(rows):
            copy = y_return(k, d, my_row, row_of(d))
            copy.start()
            sends.append(copy)
        zs = pl.ds(k * zc, zc)
        own["yr", k] = own_copy(
            ysend.at[zs, pl.ds(my_row * ylen, ylen)], yhome.at[my_row, zs],
            Y_CHUNKS + Z_CHUNKS + k)

    def z_terms(k):
        own["zf", k].wait()
        for d in order(cols):
            z_forward(k, d, col_of(cols - d), my_col).wait_recv()

        @pl.loop(k * yc, (k + 1) * yc)
        def _(y):
            s = pz[y, 0]
            w = pz[y, 1].astype(jnp.float32)
            flux = (w * s.astype(jnp.float32)).astype(jnp.bfloat16)
            term = pair_term(w, dot(m1z[...], s), dot(m1z[...], flux), dot(m2z[...], s))
            zsend[y] = term.astype(jnp.bfloat16)

        for d in order(cols):
            copy = z_return(k, d, my_col, col_of(d))
            copy.start()
            sends.append(copy)
        own["zr", k] = own_copy(
            zsend.at[pl.ds(k * yc, yc), pl.ds(my_col * zlen, zlen)],
            zhome.at[pl.ds(my_col * yb + k * yc, yc)],
            2 * Y_CHUNKS + Z_CHUNKS + k)

    y_terms(0)
    for k in range(Z_CHUNKS):
        z_terms(k)
    for k in range(1, Y_CHUNKS):
        y_terms(k)

    for k in range(Z_CHUNKS):
        own["zr", k].wait()
        for d in order(cols):
            z_return(k, d, col_of(cols - d), my_col).wait_recv()

    @pl.loop(0, ylen)
    def _(y):
        span = pl.ds(pl.multiple_of(y * zlen, zlen), zlen)
        for b in range(blocks):
            acc[b, span] += zhome[y, :, lanes(b)].astype(jnp.float32)

    for k in range(Y_CHUNKS):
        own["yr", k].wait()
        for d in order(rows):
            y_return(k, d, row_of(rows - d), my_row).wait_recv()

        @pl.loop(k * zc, (k + 1) * zc)
        def _(z):
            for b in range(blocks):
                span = pl.ds(z, ylen, stride=zlen)
                acc[b, span, :] = acc[b, span, :] + yhome[b, z].astype(jnp.float32)

    stores = []
    for b in range(blocks):
        copy = pltpu.make_async_copy(acc.at[b], out.at[:, lanes(b)], in_sem.at[b])
        copy.start()
        stores.append(copy)
    for copy in sends:
        copy.wait_send()
    for copy in stores:
        copy.wait()


def fused(rows, cols, scalars, velocity, *matrices):
    _, ylen, zlen, xlen = scalars.shape
    blocks = xlen // LANES
    points = ylen * zlen
    yb = ylen // cols
    bf, f32 = jnp.bfloat16, jnp.float32
    sems = pltpu.SemaphoreType.DMA
    flops = 6 * points * xlen * (xlen + ylen * rows + zlen * cols)
    result = pl.pallas_call(
        functools.partial(kernel, rows, cols),
        out_shape=jax.ShapeDtypeStruct((points, xlen), f32),
        in_specs=[pl.BlockSpec(memory_space=pl.ANY)] * 8,
        out_specs=pl.BlockSpec(memory_space=pl.ANY),
        scratch_shapes=[
            pltpu.VMEM((blocks, points, LANES), f32),
            pltpu.VMEM((blocks, ylen, zlen, LANES), bf),
            pltpu.VMEM((blocks, points, LANES), f32),
            pltpu.VMEM((blocks, zlen, 2, ylen, LANES), bf),
            pltpu.VMEM((zlen, 2, ylen * rows, LANES), bf),
            pltpu.VMEM((zlen, ylen * rows, LANES), bf),
            pltpu.VMEM((blocks, zlen, ylen, LANES), bf),
            pltpu.VMEM((ylen, 2, zlen, xlen), bf),
            pltpu.VMEM((ylen, zlen, xlen), bf),
            pltpu.VMEM((yb, 2, zlen * cols, xlen), bf),
            pltpu.VMEM((yb, zlen * cols, xlen), bf),
            pltpu.VMEM((ylen, zlen, xlen), bf),
            *[pltpu.VMEM(m.shape, bf) for m in matrices],
            sems((2 * blocks + 8,)),
            sems((2 * (Y_CHUNKS + Z_CHUNKS),)),
            *[sems((Y_CHUNKS, rows - 1))] * 4,
            *[sems((Z_CHUNKS, cols - 1))] * 4,
        ],
        compiler_params=pltpu.CompilerParams(
            collective_id=0, has_side_effects=True, vmem_limit_bytes=56 * 1024 * 1024),
        cost_estimate=pl.CostEstimate(
            flops=flops, bytes_accessed=14 * points * xlen, transcendentals=0),
    )(scalars.reshape(points, xlen), velocity, *matrices)
    return result.reshape(scalars.shape)


def fits(rows, cols, shape):
    count, ylen, zlen, xlen = shape
    return (
        count == 1 and rows > 1 and cols > 1
        and xlen == LANES * rows
        and ylen % (16 * Z_CHUNKS) == 0 and ylen % (cols * Z_CHUNKS) == 0
        and zlen % 16 == 0 and zlen % Y_CHUNKS == 0
        and ylen * zlen * xlen <= 1 << 20
    )


def solution(mesh):
    rows, cols = mesh.shape["row"], mesh.shape["col"]

    def step(scalars, *rest):
        if fits(rows, cols, scalars.shape):
            return fused(rows, cols, scalars, *rest)
        return body(scalars, *rest)

    split = P(None, "row", "col", None)
    return jax.shard_map(
        step,
        mesh=mesh,
        in_specs=(split, split, P(), P(), P(), P(), P(), P()),
        out_specs=split,
        check_vma=False,
    )
```

profile of v0, /device:TPU:0, one launch (start us, length us, event | category | flops | bytes accessed | tf_op | source)
XLA Modules:
  0.0 154.9 jit_solution(7349496892948397279)
XLA Ops:
  0.0 149.9 %shard_map.82 = f32[2048,512]{1,0:T(8,128)} custom-call(f32[2048,512]{1,0:T(8,128)} %bitcast.3, bf16[3,64,32,512]{3,2,1,0:T(8,128)(2,1)} %vel.1, bf16[512,512]{1,0:T(8,128)(2,1)} %f1x.1, bf16[512,512]{1,0:T(8,128)(2,1)} %f2x.1, bf16[256,256]{1,0:T(8,128)(2,1)} %f1y.1, bf16[256,256]{1,0:T(8,128)(2,1)} %f2y.1, bf16[256,256]{1,0:T(8,128)(2,1)} %f1z.1, ...), custom_call_target="tpu_custom_call" | custom-call | flops 6442450944 | bytes 14680064 | tf_op jit(solution)/shard_map/pallas_call | solution.py:337
  149.9 5.0 %copy.10 = f32[1,64,32,512]{3,2,1,0:T(8,128)} copy(f32[1,64,32,512]{3,2,1,0:T(8,128)} %bitcast.2) | data formatting | bytes 8388608
where the time goes:
time: 155 us
  Pallas kernels  150 us (97%)
  local copies, waits for them, and re-layouts  5.01 us (3%)
    pallas_call x1, Pallas kernels, fused(): pl.pallas_call(functools.partial(kernel, rows, cols), out_shape=jax.Shape...  150 us
    unnamed x1, local copies, waits for them, and re-layouts  5.01 us

commit v1 on v0

--- a/solution.py
+++ b/solution.py
@@ -12,7 +12,7 @@
 MESH = pl.DeviceIdType.MESH
 LANES = 128
 
-Y_CHUNKS = 4
+Y_CHUNKS = 8
 Z_CHUNKS = 2
 
 
@@ -121,11 +121,6 @@
 
     scal_in = [load(scal.at[:, lanes(b)], acc.at[b]) for b in range(blocks)]
     v_in = [load(vel.at[1, :, :, lanes(b)], vb.at[b]) for b in range(blocks)]
-    w_in = load(vel.at[2], sw.at[:, 1])
-    u_in = load(vel.at[0], ub)
-    x_in = [load(f1x, m1x), load(f2x, m2x)]
-    y_in = [load(f1y, m1y), load(f2y, m2y)]
-    z_in = [load(f1z, m1z), load(f2z, m2z)]
 
     barrier = pltpu.get_barrier_semaphore()
     for d in range(1, rows):
@@ -133,12 +128,12 @@
     for d in range(1, cols):
         pl.semaphore_signal(barrier, inc=1, device_id=(my_row, col_of(d)), device_id_type=MESH)
 
-    def y_forward(k, d, sender, receiver):
+    def y_forward(k, part, d, sender, receiver):
         zs = pl.ds(k * zc, zc)
         return pltpu.make_async_remote_copy(
-            src_ref=turned.at[receiver, zs],
-            dst_ref=py.at[zs, :, pl.ds(sender * ylen, ylen)],
-            send_sem=yf_send.at[k, d - 1], recv_sem=yf_recv.at[k, d - 1],
+            src_ref=turned.at[part, receiver, zs],
+            dst_ref=py.at[part, zs, pl.ds(sender * ylen, ylen)],
+            send_sem=yf_send.at[k, part, d - 1], recv_sem=yf_recv.at[k, part, d - 1],
             device_id=(row_of(d), my_col), device_id_type=MESH)
 
     def y_return(k, d, sender, receiver):
@@ -168,7 +163,40 @@
         copy.start()
         return copy
 
-    for copy in scal_in + v_in:
+    own = {}
+    sends = []
+
+    def order(n):
+        return range(1, n)
+
+    def turn_and_send_y(k, part):
+        field = vf if part else acc
+
+        @pl.loop(k * zc, (k + 1) * zc)
+        def _(z):
+            for b in range(blocks):
+                turned[part, b, z] = field[b, pl.ds(z, ylen, stride=zlen), :].astype(jnp.bfloat16)
+
+        if k == 0 and part == 0:
+            pl.semaphore_wait(barrier, rows + cols - 2)
+        for d in order(rows):
+            copy = y_forward(k, part, d, my_row, row_of(d))
+            copy.start()
+            sends.append(copy)
+        zs = pl.ds(k * zc, zc)
+        own["yf", k, part] = own_copy(
+            turned.at[part, my_row, zs], py.at[part, zs, pl.ds(my_row * ylen, ylen)], 2 * k + part)
+
+    for copy in scal_in:
+        copy.wait()
+    turn_and_send_y(0, 0)
+    w_in = load(vel.at[2], sw.at[:, 1])
+    u_in = load(vel.at[0], ub)
+    x_in = [load(f1x, m1x), load(f2x, m2x)]
+    y_in = [load(f1y, m1y), load(f2y, m2y)]
+    z_in = [load(f1z, m1z), load(f2z, m2z)]
+    turn_and_send_y(1, 0)
+    for copy in v_in:
         copy.wait()
 
     @pl.loop(0, ylen)
@@ -177,30 +205,8 @@
         for b in range(blocks):
             vf[b, span] = vb[b, y].astype(jnp.float32)
 
-    own = {}
-    sends = []
-
-    def order(n):
-        return range(n - 1, 0, -1)
-
-    def turn_and_send_y(k):
-        @pl.loop(k * zc, (k + 1) * zc)
-        def _(z):
-            for b in range(blocks):
-                turned[b, z, 0] = acc[b, pl.ds(z, ylen, stride=zlen), :].astype(jnp.bfloat16)
-                turned[b, z, 1] = vf[b, pl.ds(z, ylen, stride=zlen), :].astype(jnp.bfloat16)
-
-        if k == 0:
-            pl.semaphore_wait(barrier, rows + cols - 2)
-        for d in order(rows):
-            copy = y_forward(k, d, my_row, row_of(d))
-            copy.start()
-            sends.append(copy)
-        zs = pl.ds(k * zc, zc)
-        own["yf", k] = own_copy(
-            turned.at[my_row, zs], py.at[zs, :, pl.ds(my_row * ylen, ylen)], k)
-
-    turn_and_send_y(0)
+    turn_and_send_y(0, 1)
+    turn_and_send_y(1, 1)
 
     @pl.loop(0, ylen)
     def _(y):
@@ -216,9 +222,10 @@
             sends.append(copy)
         own["zf", k] = own_copy(
             sw.at[pl.ds(my_col * yb + k * yc, yc)],
-            pz.at[pl.ds(k * yc, yc), :, pl.ds(my_col * zlen, zlen)], Y_CHUNKS + k)
-    for k in range(1, Y_CHUNKS):
-        turn_and_send_y(k)
+            pz.at[pl.ds(k * yc, yc), :, pl.ds(my_col * zlen, zlen)], 2 * Y_CHUNKS + k)
+    for k in range(2, Y_CHUNKS):
+        for part in range(2):
+            turn_and_send_y(k, part)
 
     u_in.wait()
     for copy in x_in:
@@ -243,14 +250,15 @@
         copy.wait()
 
     def y_terms(k):
-        own["yf", k].wait()
-        for d in order(rows):
-            y_forward(k, d, row_of(rows - d), my_row).wait_recv()
+        for part in range(2):
+            own["yf", k, part].wait()
+            for d in order(rows):
+                y_forward(k, part, d, row_of(rows - d), my_row).wait_recv()
 
         @pl.loop(k * zc, (k + 1) * zc)
         def _(z):
-            s = py[z, 0]
-            v = py[z, 1].astype(jnp.float32)
+            s = py[0, z]
+            v = py[1, z].astype(jnp.float32)
             flux = (v * s.astype(jnp.float32)).astype(jnp.bfloat16)
             both = dot(m1y[...], jnp.concatenate([s, flux], axis=1))
             term = pair_term(v, both[:, :LANES], both[:, LANES:], dot(m2y[...], s))
@@ -263,7 +271,7 @@
         zs = pl.ds(k * zc, zc)
         own["yr", k] = own_copy(
             ysend.at[zs, pl.ds(my_row * ylen, ylen)], yhome.at[my_row, zs],
-            Y_CHUNKS + Z_CHUNKS + k)
+            2 * Y_CHUNKS + Z_CHUNKS + k)
 
     def z_terms(k):
         own["zf", k].wait()
@@ -285,7 +293,7 @@
         own["zr", k] = own_copy(
             zsend.at[pl.ds(k * yc, yc), pl.ds(my_col * zlen, zlen)],
             zhome.at[pl.ds(my_col * yb + k * yc, yc)],
-            2 * Y_CHUNKS + Z_CHUNKS + k)
+            3 * Y_CHUNKS + Z_CHUNKS + k)
 
     y_terms(0)
     for k in range(Z_CHUNKS):
@@ -343,8 +351,8 @@
             pltpu.VMEM((blocks, points, LANES), f32),
             pltpu.VMEM((blocks, ylen, zlen, LANES), bf),
             pltpu.VMEM((blocks, points, LANES), f32),
-            pltpu.VMEM((blocks, zlen, 2, ylen, LANES), bf),
-            pltpu.VMEM((zlen, 2, ylen * rows, LANES), bf),
+            pltpu.VMEM((2, blocks, zlen, ylen, LANES), bf),
+            pltpu.VMEM((2, zlen, ylen * rows, LANES), bf),
             pltpu.VMEM((zlen, ylen * rows, LANES), bf),
             pltpu.VMEM((blocks, zlen, ylen, LANES), bf),
             pltpu.VMEM((ylen, 2, zlen, xlen), bf),
@@ -354,15 +362,17 @@
             pltpu.VMEM((ylen, zlen, xlen), bf),
             *[pltpu.VMEM(m.shape, bf) for m in matrices],
             sems((2 * blocks + 8,)),
-            sems((2 * (Y_CHUNKS + Z_CHUNKS),)),
-            *[sems((Y_CHUNKS, rows - 1))] * 4,
+            sems((3 * Y_CHUNKS + 2 * Z_CHUNKS,)),
+            *[sems((Y_CHUNKS, 2, rows - 1))] * 2,
+            *[sems((Y_CHUNKS, rows - 1))] * 2,
             *[sems((Z_CHUNKS, cols - 1))] * 4,
         ],
         compiler_params=pltpu.CompilerParams(
-            collective_id=0, has_side_effects=True, vmem_limit_bytes=56 * 1024 * 1024),
+            collective_id=0, has_side_effects=True, vmem_limit_bytes=47 * 1024 * 1024),
         cost_estimate=pl.CostEstimate(
             flops=flops, bytes_accessed=14 * points * xlen, transcendentals=0),
-    )(scalars.reshape(points, xlen), velocity, *matrices)
+    )(scalars.reshape(points, xlen), velocity,
+      *[pltpu.with_memory_space_constraint(m, pltpu.HBM) for m in matrices])
     return result.reshape(scalars.shape)
 
 
@@ -371,7 +381,7 @@
     return (
         count == 1 and rows > 1 and cols > 1
         and xlen == LANES * rows
-        and ylen % (16 * Z_CHUNKS) == 0 and ylen % (cols * Z_CHUNKS) == 0
+        and Y_CHUNKS > 1 and ylen % 16 == 0 and ylen % (cols * Z_CHUNKS) == 0
         and zlen % 16 == 0 and zlen % Y_CHUNKS == 0
         and ylen * zlen * xlen <= 1 << 20
     )

time: 155 us -> 147 us (0.948)
  Pallas kernels: 150 us -> 145 us
  local copies, waits for them, and re-layouts: 5.01 us -> 2.02 us
    pallas_call x1, Pallas kernels: 150 us -> 145 us  [fused(): pl.pallas_call(functools.partial(kernel, rows, cols), out_shape=jax.Shape...]
    unnamed x1, local copies, waits for them, and re-layouts: 5.01 us -> 2.02 us
where the time goes in v1:
time: 147 us
  Pallas kernels  145 us (99%)
  local copies, waits for them, and re-layouts  2.02 us (1%)
    pallas_call x1, Pallas kernels, fused(): pl.pallas_call(functools.partial(kernel, rows, cols), out_shape=jax.Shape...  145 us

profile of v1, /device:TPU:0, one launch (start us, length us, event | category | flops | bytes accessed | tf_op | source)
XLA Modules:
  0.0 147.3 jit_solution(322084374393195084)
XLA Ops:
  0.0 145.3 %shard_map.82 = f32[2048,512]{1,0:T(8,128)S(1)} custom-call(f32[2048,512]{1,0:T(8,128)} %bitcast.3, bf16[3,64,32,512]{3,2,1,0:T(8,128)(2,1)} %vel.1, bf16[512,512]{1,0:T(8,128)(2,1)} %f1x.1, bf16[512,512]{1,0:T(8,128)(2,1)} %f2x.1, bf16[256,256]{1,0:T(8,128)(2,1)} %f1y.1, bf16[256,256]{1,0:T(8,128)(2,1)} %f2y.1, bf16[256,256]{1,0:T(8,128)(2,1)} %f1z.1, ...), custom_call_target="tpu_custom_call" | custom-call | flops 6442450944 | bytes 14680064 | tf_op jit(solution)/shard_map/pallas_call | solution.py:345
  145.3 2.0 %copy.10 = f32[1,64,32,512]{3,2,1,0:T(8,128)} copy(f32[1,64,32,512]{3,2,1,0:T(8,128)S(1)} %bitcast.2) | data formatting | bytes 8388608

commit v2 on v1

--- a/solution.py
+++ b/solution.py
@@ -312,22 +312,26 @@
         for b in range(blocks):
             acc[b, span] += zhome[y, :, lanes(b)].astype(jnp.float32)
 
+    stores = []
     for k in range(Y_CHUNKS):
-        own["yr", k].wait()
-        for d in order(rows):
-            y_return(k, d, row_of(rows - d), my_row).wait_recv()
-
-        @pl.loop(k * zc, (k + 1) * zc)
-        def _(z):
-            for b in range(blocks):
+        for d in range(rows):
+            sender = row_of(rows - d)
+            if d == 0:
+                own["yr", k].wait()
+            else:
+                y_return(k, d, sender, my_row).wait_recv()
+
+            @pl.loop(k * zc, (k + 1) * zc)
+            def _(z):
                 span = pl.ds(z, ylen, stride=zlen)
-                acc[b, span, :] = acc[b, span, :] + yhome[b, z].astype(jnp.float32)
-
-    stores = []
-    for b in range(blocks):
-        copy = pltpu.make_async_copy(acc.at[b], out.at[:, lanes(b)], in_sem.at[b])
-        copy.start()
-        stores.append(copy)
+                acc[sender, span, :] = acc[sender, span, :] + yhome[sender, z].astype(jnp.float32)
+
+            if k == Y_CHUNKS - 1:
+                block = pl.ds(pl.multiple_of(sender * LANES, LANES), LANES)
+                copy = pltpu.make_async_copy(acc.at[sender], out.at[:, block], in_sem.at[d])
+                copy.start()
+                stores.append(copy)
+
     for copy in sends:
         copy.wait_send()
     for copy in stores:

time: 147 us -> 147 us (level)
  no operation moved by 1% of the time
where the time goes in v2:
time: 147 us
  Pallas kernels  145 us (99%)
  local copies, waits for them, and re-layouts  2.02 us (1%)
    pallas_call x1, Pallas kernels, fused(): pl.pallas_call(functools.partial(kernel, rows, cols), out_shape=jax.Shape...  145 us

profile of v2, /device:TPU:0, one launch (start us, length us, event | category | flops | bytes accessed | tf_op | source)
XLA Modules:
  0.0 146.7 jit_solution(4933453956966331621)
XLA Ops:
  0.0 144.7 %shard_map.82 = f32[2048,512]{1,0:T(8,128)S(1)} custom-call(f32[2048,512]{1,0:T(8,128)} %bitcast.3, bf16[3,64,32,512]{3,2,1,0:T(8,128)(2,1)} %vel.1, bf16[512,512]{1,0:T(8,128)(2,1)} %f1x.1, bf16[512,512]{1,0:T(8,128)(2,1)} %f2x.1, bf16[256,256]{1,0:T(8,128)(2,1)} %f1y.1, bf16[256,256]{1,0:T(8,128)(2,1)} %f2y.1, bf16[256,256]{1,0:T(8,128)(2,1)} %f1z.1, ...), custom_call_target="tpu_custom_call" | custom-call | flops 6442450944 | bytes 14680064 | tf_op jit(solution)/shard_map/pallas_call | solution.py:349
  144.7 2.0 %copy.10 = f32[1,64,32,512]{3,2,1,0:T(8,128)} copy(f32[1,64,32,512]{3,2,1,0:T(8,128)S(1)} %bitcast.2) | data formatting | bytes 8388608
